TPU v7x, 256 devices: a whole 4x4x8 slice. The times are simulated.
256 devices in a mesh: seq: 16 (over x, y_hi, core), dp: 16 (over z, y_lo).
Axes of the slice: x: 4, y: 4 (y_hi: 2, y_lo: 2; y = y_hi * 2 + y_lo), z: 8, core: 2. Of those that a mesh axis runs over, the one named last changes fastest.
Arguments:
- frames: bfloat16 [16, 2048, 1024], P('dp', 'seq'), may hold values from -6 to 6
- lengths: int32 [16], P('dp'), may hold values from 1024 to 2048, as said below
- stretch_sizes: int32 [16], P('dp'), may hold values from 8 to 32, as said below
- look_ahead: int32 [16], P('dp'), may hold values from 1 to 8, as said below
- norm_one: float32 [1024], replicated, may hold values from 0.5 to 1.5
- norm_two: float32 [1024], replicated, may hold values from 0.5 to 1.5
- w_query: bfloat16 [1024, 1024], replicated, may hold values from -8 to 8
- w_key: bfloat16 [1024, 1024], replicated, may hold values from -1 to 1
- w_value: bfloat16 [1024, 1024], replicated, may hold values from -0.1875 to 0.1875
- w_out: bfloat16 [1024, 1024], replicated, may hold values from -0.1875 to 0.1875
- conv_kernel: bfloat16 [31, 1024], replicated, may hold values from -1 to 1
Outputs:
- full_output: bfloat16 [16, 2048, 1024], P('dp', 'seq')
- stretch_output: bfloat16 [16, 2048, 1024], P('dp', 'seq')
- kernel_grad: float32 [31, 1024], replicated
Inputs may be any that keep to these rules, and one draw needn't show every extreme that they name: `lengths`: utterance 0 has all 2048 frames. `stretch_sizes`: utterance 0 has stretch size 32. `look_ahead`: utterance 0 has preview 8.
All inputs are finite; a program needn't handle non-finite values.
Results may differ from a plain program's by a relative error of at most 0.0045.
The roundings to bfloat16 on the way count: a program that leaves them out, or rounds other values in their place, can miss the bound.
Values may be sent and summed in bfloat16 or wider, within the bound.
No kernel may reach another device: no remote copies, remote signals or barrier semaphores. Data moves between devices by JAX's collectives and lax.ppermute only.
A program may use at most 128 MiB of HBM per device.

v0:
```python
import math
import jax
import jax.numpy as jnp
from jax import lax
from jax.sharding import PartitionSpec as P

HEADS = 16
KERNEL = 31
LEFT = 64
HALO = 128
EPSILON = 1e-05
FLOOR_SCORE = -1e30


def with_halo(value, sides, width):
    for axis, dim in sides:
        size, length = (lax.axis_size(axis), value.shape[dim])
        up = [(i, (i + 1) % size) for i in range(size - 1)]
        down = [(j, i) for i, j in up]
        last = lax.slice_in_dim(value, length - width, length, axis=dim)
        leading = lax.slice_in_dim(value, 0, width, axis=dim)
        before = lax.ppermute(last, axis, up)
        after = lax.ppermute(leading, axis, down)
        value = jnp.concatenate([before, value, after], axis=dim)
    return value


def shifted(value, axis, by):
    length = lax.axis_size(axis)
    pairs = [(i, i + by) for i in range(length) if 0 <= i + by < length]
    return lax.ppermute(value, axis, pairs)


def layer_norm(values, gain_vector):
    values = values.astype(jnp.float32)
    center = values - jnp.mean(values, axis=-1, keepdims=True)
    spread = jnp.mean(center * center, axis=-1, keepdims=True)
    return center * lax.rsqrt(spread + EPSILON) * gain_vector


def fresh_state(row_count, head_count, depth_count):
    return (
        jnp.full((head_count, row_count), FLOOR_SCORE, jnp.float32),
        jnp.zeros((head_count, row_count), jnp.float32),
        jnp.zeros((row_count, head_count * depth_count), jnp.float32),
    )


def finish_state(state):
    highest, totals, summed = state
    row_count = summed.shape[0]
    head_count = totals.shape[0]
    mixed = summed.reshape(row_count, head_count, -1) / totals.T[:, :, None]
    return mixed.reshape(row_count, -1).astype(jnp.bfloat16)


def fold_keys(state, query3, query_pos, key3, value3, key_start, length, scale):
    highest, totals, summed = state
    key_count = key3.shape[0]
    scores = jnp.einsum("qhe,khe->hqk", query3, key3, preferred_element_type=jnp.float32) * scale
    key_pos = key_start + jnp.arange(key_count, dtype=jnp.int32)
    visible = (key_pos[None, :] < length) | (key_pos[None, :] == query_pos[:, None])
    scores = jnp.where(visible[None], scores, FLOOR_SCORE)
    new_high = jnp.maximum(highest, jnp.max(scores, axis=-1))
    factor = jnp.exp(highest - new_high)
    expo = jnp.where(visible[None], jnp.exp(scores - new_high[:, :, None]), 0.0)
    totals = totals * factor + jnp.sum(expo, axis=-1)
    adding = jnp.einsum(
        "hqk,khe->qhe", expo.astype(jnp.bfloat16), value3, preferred_element_type=jnp.float32
    )
    row_count, head_count, depth_count = adding.shape
    summed = summed.reshape(row_count, head_count, depth_count) * factor.T[:, :, None] + adding
    return (new_high, totals, summed.reshape(row_count, head_count * depth_count))


def fold_blocks(state, query3, query_pos, keys3, values3, length, scale):
    key_count = keys3.shape[0]
    block_width = math.gcd(key_count, 256)
    number = key_count // block_width
    key_blocks = keys3.reshape(number, block_width, keys3.shape[1], keys3.shape[2])
    value_blocks = values3.reshape(number, block_width, values3.shape[1], values3.shape[2])

    def advance(carry, inputs):
        index, key_block, value_block = inputs
        return (
            fold_keys(
                carry, query3, query_pos, key_block, value_block, index * block_width, length, scale
            ),
            None,
        )

    state, _ = lax.scan(
        advance, state, (jnp.arange(number, dtype=jnp.int32), key_blocks, value_blocks)
    )
    return state


def windowed(query3, key_ext3, value_ext3, first_pos, length, stretch, lookup, scale):
    query_count = query3.shape[0]
    block_rows = min(query_count, 512)
    number = query_count // block_rows
    span = block_rows + 2 * HALO

    def one_block(index):
        start = index * block_rows
        query_pos = first_pos + start + jnp.arange(block_rows, dtype=jnp.int32)
        key_pos = first_pos + start - HALO + jnp.arange(span, dtype=jnp.int32)
        begin = query_pos // stretch * stretch
        inside = (key_pos[None, :] >= begin[:, None] - LEFT) & (
            key_pos[None, :] < begin[:, None] + stretch + lookup
        )
        inside = inside & (key_pos[None, :] >= 0) & (key_pos[None, :] < length)
        visible = inside | (key_pos[None, :] == query_pos[:, None])
        scores = (
            jnp.einsum("qhe,khe->hqk", query3, key_ext3, preferred_element_type=jnp.float32) * scale
        )
        scores = jnp.where(visible[None], scores, FLOOR_SCORE)
        highest = jnp.max(scores, axis=-1, keepdims=True)
        expo = jnp.where(visible[None], jnp.exp(scores - highest), 0.0)
        totals = jnp.sum(expo, axis=-1)
        mixed = jnp.einsum(
            "hqk,khe->qhe",
            expo.astype(jnp.bfloat16),
            value_ext3,
            preferred_element_type=jnp.float32,
        )
        return (mixed / totals.T[:, :, None]).reshape(block_rows, -1).astype(jnp.bfloat16)

    return lax.map(one_block, jnp.arange(number, dtype=jnp.int32)).reshape(query_count, -1)


def per_device(
    frames,
    lengths,
    stretch_sizes,
    look_ahead,
    norm_one,
    norm_two,
    w_query,
    w_key,
    w_value,
    w_out,
    conv_kernel,
):
    source = frames[0]
    row_count, model_width = source.shape
    head_count = HEADS
    depth_count = model_width // head_count
    scale = float(depth_count) ** (-0.5)
    seq_place = lax.axis_index("seq")
    length = lengths[0]
    stretch = stretch_sizes[0]
    lookup = look_ahead[0]
    first_pos = seq_place * row_count
    query_pos = first_pos + jnp.arange(row_count, dtype=jnp.int32)
    normed = layer_norm(source, norm_one).astype(jnp.bfloat16)
    query = jnp.dot(normed, w_query, preferred_element_type=jnp.float32).astype(jnp.bfloat16)
    key_rows = jnp.dot(normed, w_key, preferred_element_type=jnp.float32).astype(jnp.bfloat16)
    value_rows = jnp.dot(normed, w_value, preferred_element_type=jnp.float32).astype(jnp.bfloat16)
    query3 = query.reshape(row_count, head_count, depth_count)
    key_piece = lax.all_gather(key_rows, "seq", axis=0, tiled=True)
    value_piece = lax.all_gather(value_rows, "seq", axis=0, tiled=True)
    piece_rows = key_piece.shape[0]
    state = fold_blocks(
        fresh_state(row_count, head_count, depth_count),
        query3,
        query_pos,
        key_piece.reshape(piece_rows, head_count, depth_count),
        value_piece.reshape(piece_rows, head_count, depth_count),
        length,
        scale,
    )
    context_full = finish_state(state)
    stacked = jnp.stack([key_rows, value_rows])
    extended = with_halo(stacked, (("seq", 1),), HALO)
    context_stretch = windowed(
        query3,
        extended[0].reshape(-1, head_count, depth_count),
        extended[1].reshape(-1, head_count, depth_count),
        first_pos,
        length,
        stretch,
        lookup,
        scale,
    )
    valid = (query_pos < length).astype(jnp.float32)
    kernel_taps = conv_kernel.astype(jnp.float32)
    projected = jnp.dot(
        jnp.concatenate([context_full, context_stretch], axis=0),
        w_out,
        preferred_element_type=jnp.float32,
    )
    residual_full = source.astype(jnp.float32) + projected[:row_count]
    residual_stretch = source.astype(jnp.float32) + projected[row_count:]
    input_full = (layer_norm(residual_full, norm_two) * valid[:, None]).astype(jnp.bfloat16)
    input_stretch = (layer_norm(residual_stretch, norm_two) * valid[:, None]).astype(jnp.bfloat16)
    padded_full = with_halo(input_full, (("seq", 0),), KERNEL // 2)
    carried = shifted(input_stretch[row_count - (KERNEL - 1) :], "seq", 1)
    padded_stretch = jnp.concatenate([carried, input_stretch], axis=0)
    conv_full = jnp.zeros((row_count, model_width), jnp.float32)
    conv_stretch = jnp.zeros((row_count, model_width), jnp.float32)
    for offset in range(KERNEL):
        conv_full = conv_full + kernel_taps[offset] * padded_full[
            offset : offset + row_count
        ].astype(jnp.float32)
        conv_stretch = conv_stretch + kernel_taps[offset] * padded_stretch[
            offset : offset + row_count
        ].astype(jnp.float32)
    output_full = residual_full + jax.nn.silu(conv_full)
    output_stretch = residual_stretch + jax.nn.silu(conv_stretch)
    push = (
        2.0 * (output_stretch - output_full) * valid[:, None] / jnp.sqrt(length.astype(jnp.float32))
    )
    sigma = jax.nn.sigmoid(conv_stretch)
    slope = push * sigma * (1.0 + conv_stretch * (1.0 - sigma))
    grad_local = jnp.stack(
        [
            jnp.sum(slope * padded_stretch[offset : offset + row_count].astype(jnp.float32), axis=0)
            for offset in range(KERNEL)
        ]
    )
    kernel_grad = lax.psum(grad_local, ("seq", "dp"))
    return (
        output_full.astype(jnp.bfloat16)[None],
        output_stretch.astype(jnp.bfloat16)[None],
        kernel_grad,
    )


def solution(mesh):
    in_specs = (P("dp", "seq", None), P("dp"), P("dp"), P("dp"), P(), P(), P(), P(), P(), P(), P())
    out_specs = (P("dp", "seq", None), P("dp", "seq", None), P())
    return jax.shard_map(
        per_device, mesh=mesh, in_specs=in_specs, out_specs=out_specs, check_vma=False
    )
```

profile of v0, /device:TPU:8, one launch (start us, length us, event | category | flops | bytes accessed | tf_op | source)
XLA Modules:
  0.0 529.4 jit_solution(953079403688141178)
XLA Ops:
  9.7 2.9 convolution_convert_fusion.2
  12.7 2.8 convolution_convert_fusion
  17.4 2.6 collective-permute-start
  33.6 3.8 fusion.188
  37.4 2.9 fusion.36
  40.3 40.4 %all-gather.3.cloned.1.call-done = bf16[2048,1024]{1,0:T(8,128)(2,1)} async-done(((bf16[128,1024]{1,0:T(8,128)(2,1)}), bf16[2048,1024]{1,0:T(8,128)(2,1)}) %all-gather.3.cloned.1.call-update) | async-done | bytes 4194320 | tf_op jit(solution)/shard_map/all_gather | solution.py:161
  80.8 11.6 %reshape.276 = bf16[8,256,16,64]{3,2,1,0:T(8,128)(2,1)} reshape(bf16[2048,1024]{1,0:T(8,128)(2,1)} %all-gather.3.cloned.1.call-done) | data formatting | bytes 8388608 | tf_op jit(solution)/shard_map/reshape;reshape | solution.py:80
  92.3 10.4 %copy.25 = bf16[8,256,16,64]{1,3,2,0:T(8,128)(2,1)} copy(bf16[8,256,16,64]{3,2,1,0:T(8,128)(2,1)} %reshape.276) | data formatting | bytes 8388608
  102.7 41.3 %all-gather.5.cloned.1.call-done = bf16[2048,1024]{1,0:T(8,128)(2,1)} async-done(((bf16[128,1024]{1,0:T(8,128)(2,1)}), bf16[2048,1024]{1,0:T(8,128)(2,1)}) %all-gather.5.cloned.1.call-update) | async-done | bytes 4194320 | tf_op jit(solution)/shard_map/all_gather | solution.py:162
  144.0 11.6 %reshape.277 = bf16[8,256,16,64]{3,2,1,0:T(8,128)(2,1)} reshape(bf16[2048,1024]{1,0:T(8,128)(2,1)} %all-gather.5.cloned.1.call-done) | data formatting | bytes 8388608 | tf_op jit(solution)/shard_map/reshape;reshape | solution.py:81
  155.6 10.3 %copy.26 = bf16[8,256,16,64]{1,3,2,0:T(8,128)(2,1)} copy(bf16[8,256,16,64]{3,2,1,0:T(8,128)(2,1)} %reshape.277) | data formatting | bytes 8388608
  166.0 65.6 %while.5 = (s32[]{:T(128)}, f32[16,128]{1,0:T(8,128)S(1)}, f32[16,128]{1,0:T(8,128)S(1)}, f32[128,1024]{0,1:T(8,128)S(1)}, s32[8]{0:T(128)S(1)}, /*index=5*/s32[...) while((s32[]{:T(128)}, f32[16,128]{1,0:T(8,128)S(1)}, ...), condition=%wide.region_5.6_spmd.clone, body=%wide.region_2.5_spmd.clone.sunk | while | flops 141374336 | bytes 17306316 | solution.py:92
  168.0 2.9 fusion.211
  171.0 2.6 fusion.215
  176.2 2.9 fusion.211
  179.2 2.6 fusion.215
  184.4 2.9 fusion.211
  187.4 2.6 fusion.215
  192.6 2.9 fusion.211
  195.6 2.6 fusion.215
  200.8 2.9 fusion.211
  203.8 2.6 fusion.215
  209.0 2.9 fusion.211
  212.0 2.6 fusion.215
  217.2 2.9 fusion.211
  220.2 2.6 fusion.215
  225.4 2.9 fusion.211
  228.4 2.6 fusion.215
  237.8 3.8 collective-permute-start.2
  245.1 21.2 %fusion.106 = (f32[1024]{0:T(1024)S(1)}, f32[1024]{0:T(1024)S(1)}, f32[1024]{0:T(1024)S(1)}, f32[1024]{0:T(1024)S(1)}, f32[1024]{0:T(1024)S(1)}, /*index=5*/f32[...) fusion(bf16[128,1024]{1,0:T(8,128)(2,1)} %copy-done.3, ...), kind=kLoop, calls=%fused_computation.235 | loop fusion | flops 57138176 | bytes 3432964 | tf_op jit(solution)/shard_map/reduce_sum | solution.py:218
  269.0 4.7 stack.139
  275.7 245.6 %all-reduce.2.cloned.1.call-done = f32[31,1024]{1,0:T(8,128)} async-done(((f32[31,1024]{1,0:T(8,128)}), f32[31,1024]{1,0:T(8,128)}) %all-reduce.2.cloned.1.call-update) | async-done | bytes 126992 | tf_op jit(solution)/shard_map/psum | solution.py:222
  (166 shorter events, 47.3 us)
Async XLA Ops:
  7.2 224.5 %copy-start = (bf16[1024,1024]{1,0:T(8,128)(2,1)S(1)}, bf16[1024,1024]{1,0:T(8,128)(2,1)}, u32[]{:S(2)}) copy-start(bf16[1024,1024]{1,0:T(8,128)(2,1)} %param.22) | copy-start | bytes 6291460
  7.2 5.5 %copy-start.2 = (bf16[1,128,1024]{2,1,0:T(8,128)(2,1)S(1)}, bf16[1,128,1024]{2,1,0:T(8,128)(2,1)}, u32[]{:S(2)}) copy-start(bf16[1,128,1024]{2,1,0:T(8,128)(2,1)} %param.13) | copy-start | bytes 786436
  7.2 5.5 %copy-start.10 = (f32[1024]{0:T(1024)S(1)}, f32[1024]{0:T(1024)}, u32[]{:S(2)}) copy-start(f32[1024]{0:T(1024)} %param.17) | copy-start | bytes 12292
  7.2 73.6 %all-gather.3.cloned.1.call-start = ((), (), s32[]{:S(2)}) async-start(), calls=%async_computation | async-start | bytes 4456448 | tf_op jit(solution)/shard_map/all_gather | solution.py:161
  12.6 3.0 copy-start.5
  12.6 131.4 %all-gather.5.cloned.1.call-start = ((), (), s32[]{:S(2)}) async-start(), calls=%async_computation.1 | async-start | bytes 4456448 | tf_op jit(solution)/shard_map/all_gather | solution.py:162
  15.5 505.8 %all-reduce.2.cloned.1.call-start = ((), (), s32[]{:S(2)}) async-start(), calls=%async_computation.2 | async-start | bytes 262144 | tf_op jit(solution)/shard_map/psum | solution.py:222
  15.5 10.9 %copy-start.9 = (bf16[31,1024]{1,0:T(8,128)(2,1)S(1)}, bf16[31,1024]{1,0:T(8,128)(2,1)}, u32[]{:S(2)}) copy-start(bf16[31,1024]{1,0:T(8,128)(2,1)} %param.23) | copy-start | bytes 190468
  15.5 12.3 %copy-start.6 = (bf16[128,1024]{1,0:T(8,128)(2,1)S(1)}, bf16[128,1024]{1,0:T(8,128)(2,1)}, u32[]{:S(2)}) copy-start(bf16[128,1024]{1,0:T(8,128)(2,1)} %convolution_convert_fusion) | copy-start | bytes 786436
  17.4 10.4 %collective-permute-start = (bf16[2,128,1024]{2,1,0:T(8,128)(2,1)}, bf16[2,128,1024]{2,1,0:T(8,128)(2,1)}, u32[]{:S(2)}, u32[]{:S(2)}) collective-permute-start(bf16[2,128,1024]{2,1,0:T(8,128)(2,1)} %pad_maximum_fusion.1), channel_id=1, source_target_pairs={{0,16},{16,32},{32,48},{48,64},{64,80},{80,96},{96,112},{112,128},... | collective-permute-start | bytes 1572872 | tf_op jit(solution)/shard_map/ppermute | solution.py:22
  20.0 7.8 %collective-permute-start.1 = (bf16[2,128,1024]{2,1,0:T(8,128)(2,1)}, bf16[2,128,1024]{2,1,0:T(8,128)(2,1)}, u32[]{:S(2)}, u32[]{:S(2)}) collective-permute-start(bf16[2,128,1024]{2,1,0:T(8,128)(2,1)} %pad_maximum_fusion.1), channel_id=1, source_target_pairs={{16,0},{32,16},{48,32},{64,48},{80,64},{96,80},{112,96},{128,112},... | collective-permute-start | bytes 1572872 | tf_op jit(solution)/shard_map/ppermute | solution.py:23
  33.6 3.8 copy-start.8
  171.0 2.6 copy-start.1
  179.2 2.6 copy-start.1
  187.4 2.6 copy-start.1
  195.6 2.6 copy-start.1
  203.8 2.6 copy-start.1
  212.0 2.6 copy-start.1
  220.2 2.6 copy-start.1
  228.4 2.6 copy-start.1
  233.3 0.7 copy-start.11
  233.3 0.7 copy-start.12
  234.3 0.7 copy-start.3
  234.3 2.9 copy-start.7
  235.0 10.0 %collective-permute-start.4 = (bf16[30,1024]{1,0:T(8,128)(2,1)S(1)}, bf16[30,1024]{1,0:T(8,128)(2,1)S(1)}, u32[]{:S(2)}, u32[]{:S(2)}) collective-permute-start(bf16[30,1024]{1,0:T(8,128)(2,1)S(1)} %slice.576), channel_id=1, source_target_pairs={{0,16},{16,32},{32,48},{48,64},{64,80},{80,96},{96,112},{112,128},... | collective-permute-start | bytes 184328 | tf_op jit(solution)/shard_map/ppermute | solution.py:31
  237.8 5.7 %collective-permute-start.2 = (bf16[15,1024]{1,0:T(8,128)(2,1)}, bf16[15,1024]{1,0:T(8,128)(2,1)}, u32[]{:S(2)}, u32[]{:S(2)}) collective-permute-start(bf16[15,1024]{1,0:T(8,128)(2,1)} %get-tuple-element.207), channel_id=1, source_target_pairs={{0,16},{16,32},{32,48},{48,64},{64,80},{80,96},{96,112},{112,128},... | collective-permute-start | bytes 92168 | tf_op jit(solution)/shard_map/ppermute | solution.py:22
  241.6 3.4 collective-permute-start.3
  243.5 22.7 %copy-start.4 = (bf16[128,1024]{1,0:T(8,128)(2,1)S(1)}, bf16[128,1024]{1,0:T(8,128)(2,1)}, u32[]{:S(2)}) copy-start(bf16[128,1024]{1,0:T(8,128)(2,1)} %copy-done.3) | copy-start | bytes 786436
Sparse Core Ops, SparseCore 0:
  12.7 67.9 all-gather.2
  84.0 59.9 all-gather.4
  273.9 247.2 all-reduce.1
where the time goes:
time: 532 us; the launch traced here: 529 us
  waiting for transfers between devices  329 us (62%)
  local copies, waits for them, and re-layouts  62.4 us (12%)
  matrix products  60.6 us (11%)
  other arithmetic  44.4 us (8%)
  between operations  16.1 us (3%)
  starting transfers between devices  11.2 us (2%)
  loops' own time  5.82 us (1%)
    psum x1, waiting for transfers between devices, per_device(): kernel_grad = lax.psum(grad_local, ('seq', 'dp'))  246 us
    all_gather x1, waiting for transfers between devices, per_device(): value_piece = lax.all_gather(value_rows, 'seq', axis=0, tiled=True)  41.3 us
    all_gather x1, waiting for transfers between devices, per_device(): key_piece = lax.all_gather(key_rows, 'seq', axis=0, tiled=True)  40.4 us
    reduce_sum x4, other arithmetic, per_device(): jnp.sum(slope * padded_stretch[offset:offset + row_count].astype(jnp.floa...  24 us
    dot_general x8, matrix products, fold_keys(): jnp.einsum('qhe,khe->hqk', query3, key3, preferred_element_type=jnp.float32)  23.4 us
    unnamed x27, local copies, waits for them, and re-layouts  23.2 us
    dot_general x8, matrix products, fold_keys(): jnp.einsum('hqk,khe->qhe', expo.astype(jnp.bfloat16), value3, preferred_e...  21 us
    another operation x1, local copies, waits for them, and re-layouts, fold_blocks(): values3.reshape(number, block_width, values3.shape[1], values3.shape[2])  11.6 us
  transfers between devices with their start and end apart: 8, of which 4 were waited for; matrix products, arithmetic and copies ran while one was open for 9% of the time, Pallas kernels for 0%

commit v1 on v0

--- a/solution.py
+++ b/solution.py
@@ -219,7 +219,9 @@
             for offset in range(KERNEL)
         ]
     )
-    kernel_grad = lax.psum(grad_local, ("seq", "dp"))
+    kernel_grad = grad_local
+    for mesh_axis in ("dp", "seq"):
+        kernel_grad = lax.psum(kernel_grad, mesh_axis)
     return (
         output_full.astype(jnp.bfloat16)[None],
         output_stretch.astype(jnp.bfloat16)[None],

time: 532 us -> 569 us (1.070)
  waiting for transfers between devices: 329 us -> 365 us
    psum x1 -> x2, waiting for transfers between devices: 246 us -> 282 us  [per_device(): kernel_grad = lax.psum(kernel_grad, mesh_axis)]
  transfers between devices with their start and end apart: 8 -> 9, of which waited for: 4 -> 5; matrix products, arithmetic and copies ran while one was open for 9% -> 8% of each run, Pallas kernels for 0% -> 0%
where the time goes in v1:
time: 569 us; the launch traced here: 566 us
  waiting for transfers between devices  365 us (64%)
  local copies, waits for them, and re-layouts  62.4 us (11%)
  matrix products  60.6 us (11%)
  other arithmetic  44.4 us (8%)
  between operations  16.1 us (3%)
  starting transfers between devices  11.2 us (2%)
  loops' own time  5.82 us (1%)
    psum x2, waiting for transfers between devices, per_device(): kernel_grad = lax.psum(kernel_grad, mesh_axis)  282 us
    all_gather x1, waiting for transfers between devices, per_device(): value_piece = lax.all_gather(value_rows, 'seq', axis=0, tiled=True)  41.3 us
    all_gather x1, waiting for transfers between devices, per_device(): key_piece = lax.all_gather(key_rows, 'seq', axis=0, tiled=True)  40.4 us
    reduce_sum x4, other arithmetic, per_device(): jnp.sum(slope * padded_stretch[offset:offset + row_count].astype(jnp.floa...  24 us
    dot_general x8, matrix products, fold_keys(): jnp.einsum('qhe,khe->hqk', query3, key3, preferred_element_type=jnp.float32)  23.4 us
    unnamed x27, local copies, waits for them, and re-layouts  23.2 us
    dot_general x8, matrix products, fold_keys(): jnp.einsum('hqk,khe->qhe', expo.astype(jnp.bfloat16), value3, preferred_e...  21 us
    another operation x1, local copies, waits for them, and re-layouts, fold_blocks(): values3.reshape(number, block_width, values3.shape[1], values3.shape[2])  11.6 us
  transfers between devices with their start and end apart: 9, of which 5 were waited for; matrix products, arithmetic and copies ran while one was open for 8% of the time, Pallas kernels for 0%

profile of v1, /device:TPU:8, one launch (start us, length us, event | category | flops | bytes accessed | tf_op | source)
XLA Modules:
  0.0 565.9 jit_solution(6299350938346160483)
XLA Ops:
  9.7 2.9 convolution_convert_fusion.2
  12.7 2.8 convolution_convert_fusion
  33.6 3.8 fusion.188
  37.4 2.9 fusion.36
  40.3 40.4 %all-gather.3.cloned.1.call-done = bf16[2048,1024]{1,0:T(8,128)(2,1)} async-done(((bf16[128,1024]{1,0:T(8,128)(2,1)}), bf16[2048,1024]{1,0:T(8,128)(2,1)}) %all-gather.3.cloned.1.call-update) | async-done | bytes 4194320 | tf_op jit(solution)/shard_map/all_gather | solution.py:161
  80.8 11.6 %reshape.276 = bf16[8,256,16,64]{3,2,1,0:T(8,128)(2,1)} reshape(bf16[2048,1024]{1,0:T(8,128)(2,1)} %all-gather.3.cloned.1.call-done) | data formatting | bytes 8388608 | tf_op jit(solution)/shard_map/reshape;reshape | solution.py:80
  92.3 10.4 %copy.25 = bf16[8,256,16,64]{1,3,2,0:T(8,128)(2,1)} copy(bf16[8,256,16,64]{3,2,1,0:T(8,128)(2,1)} %reshape.276) | data formatting | bytes 8388608
  102.7 41.3 %all-gather.5.cloned.1.call-done = bf16[2048,1024]{1,0:T(8,128)(2,1)} async-done(((bf16[128,1024]{1,0:T(8,128)(2,1)}), bf16[2048,1024]{1,0:T(8,128)(2,1)}) %all-gather.5.cloned.1.call-update) | async-done | bytes 4194320 | tf_op jit(solution)/shard_map/all_gather | solution.py:162
  144.0 11.6 %reshape.277 = bf16[8,256,16,64]{3,2,1,0:T(8,128)(2,1)} reshape(bf16[2048,1024]{1,0:T(8,128)(2,1)} %all-gather.5.cloned.1.call-done) | data formatting | bytes 8388608 | tf_op jit(solution)/shard_map/reshape;reshape | solution.py:81
  155.6 10.3 %copy.26 = bf16[8,256,16,64]{1,3,2,0:T(8,128)(2,1)} copy(bf16[8,256,16,64]{3,2,1,0:T(8,128)(2,1)} %reshape.277) | data formatting | bytes 8388608
  166.0 65.6 %while.5 = (s32[]{:T(128)}, f32[16,128]{1,0:T(8,128)S(1)}, f32[16,128]{1,0:T(8,128)S(1)}, f32[128,1024]{0,1:T(8,128)S(1)}, s32[8]{0:T(128)S(1)}, /*index=5*/s32[...) while((s32[]{:T(128)}, f32[16,128]{1,0:T(8,128)S(1)}, ...), condition=%wide.region_5.6_spmd.clone, body=%wide.region_2.5_spmd.clone.sunk | while | flops 141374336 | bytes 17306316 | solution.py:92
  168.0 2.9 fusion.211
  171.0 2.6 fusion.215
  176.2 2.9 fusion.211
  179.2 2.6 fusion.215
  184.4 2.9 fusion.211
  187.4 2.6 fusion.215
  192.6 2.9 fusion.211
  195.6 2.6 fusion.215
  200.8 2.9 fusion.211
  203.8 2.6 fusion.215
  209.0 2.9 fusion.211
  212.0 2.6 fusion.215
  217.2 2.9 fusion.211
  220.2 2.6 fusion.215
  225.4 2.9 fusion.211
  228.4 2.6 fusion.215
  237.8 3.8 collective-permute-start.2
  245.1 21.2 %fusion.106 = (f32[1024]{0:T(1024)S(1)}, f32[1024]{0:T(1024)S(1)}, f32[1024]{0:T(1024)S(1)}, f32[1024]{0:T(1024)S(1)}, f32[1024]{0:T(1024)S(1)}, /*index=5*/f32[...) fusion(bf16[128,1024]{1,0:T(8,128)(2,1)} %copy-done.3, ...), kind=kLoop, calls=%fused_computation.235 | loop fusion | flops 57138176 | bytes 3432964 | tf_op jit(solution)/shard_map/reduce_sum | solution.py:218
  269.0 4.7 stack.139
  273.9 140.1 %all-reduce.3.cloned.1.call-done = f32[31,1024]{1,0:T(8,128)} async-done(((f32[31,1024]{1,0:T(8,128)}), f32[31,1024]{1,0:T(8,128)}) %all-reduce.3.cloned.1.call-update) | async-done | bytes 126992 | tf_op jit(solution)/shard_map/psum | solution.py:224
  415.9 141.9 %all-reduce.5.cloned.1.call-done = f32[31,1024]{1,0:T(8,128)} async-done(((f32[31,1024]{1,0:T(8,128)}), f32[31,1024]{1,0:T(8,128)}) %all-reduce.5.cloned.1.call-update) | async-done | bytes 126992 | tf_op jit(solution)/shard_map/psum | solution.py:224
  (169 shorter events, 49.9 us)
Async XLA Ops:
  7.2 224.5 %copy-start = (bf16[1024,1024]{1,0:T(8,128)(2,1)S(1)}, bf16[1024,1024]{1,0:T(8,128)(2,1)}, u32[]{:S(2)}) copy-start(bf16[1024,1024]{1,0:T(8,128)(2,1)} %param.22) | copy-start | bytes 6291460
  7.2 5.5 copy-start.2
  7.2 5.5 copy-start.10
  7.2 73.6 %all-gather.3.cloned.1.call-start = ((), (), s32[]{:S(2)}) async-start(), calls=%async_computation | async-start | bytes 4456448 | tf_op jit(solution)/shard_map/all_gather | solution.py:161
  12.6 3.0 copy-start.5
  12.6 131.4 %all-gather.5.cloned.1.call-start = ((), (), s32[]{:S(2)}) async-start(), calls=%async_computation.1 | async-start | bytes 4456448 | tf_op jit(solution)/shard_map/all_gather | solution.py:162
  15.5 398.5 %all-reduce.3.cloned.1.call-start = ((), (), s32[]{:S(2)}) async-start(), calls=%async_computation.2 | async-start | bytes 262144 | tf_op jit(solution)/shard_map/psum | solution.py:224
  15.5 10.9 %copy-start.9 = (bf16[31,1024]{1,0:T(8,128)(2,1)S(1)}, bf16[31,1024]{1,0:T(8,128)(2,1)}, u32[]{:S(2)}) copy-start(bf16[31,1024]{1,0:T(8,128)(2,1)} %param.23) | copy-start | bytes 190468
  15.5 12.3 %copy-start.6 = (bf16[128,1024]{1,0:T(8,128)(2,1)S(1)}, bf16[128,1024]{1,0:T(8,128)(2,1)}, u32[]{:S(2)}) copy-start(bf16[128,1024]{1,0:T(8,128)(2,1)} %convolution_convert_fusion) | copy-start | bytes 786436
  17.4 10.4 %collective-permute-start = (bf16[2,128,1024]{2,1,0:T(8,128)(2,1)}, bf16[2,128,1024]{2,1,0:T(8,128)(2,1)}, u32[]{:S(2)}, u32[]{:S(2)}) collective-permute-start(bf16[2,128,1024]{2,1,0:T(8,128)(2,1)} %pad_maximum_fusion.1), channel_id=1, source_target_pairs={{0,16},{16,32},{32,48},{48,64},{64,80},{80,96},{96,112},{112,128},... | collective-permute-start | bytes 1572872 | tf_op jit(solution)/shard_map/ppermute | solution.py:22
  20.0 7.8 %collective-permute-start.1 = (bf16[2,128,1024]{2,1,0:T(8,128)(2,1)}, bf16[2,128,1024]{2,1,0:T(8,128)(2,1)}, u32[]{:S(2)}, u32[]{:S(2)}) collective-permute-start(bf16[2,128,1024]{2,1,0:T(8,128)(2,1)} %pad_maximum_fusion.1), channel_id=1, source_target_pairs={{16,0},{32,16},{48,32},{64,48},{80,64},{96,80},{112,96},{128,112},... | collective-permute-start | bytes 1572872 | tf_op jit(solution)/shard_map/ppermute | solution.py:23
  33.6 3.8 copy-start.8
  171.0 2.6 copy-start.1
  179.2 2.6 copy-start.1
  187.4 2.6 copy-start.1
  195.6 2.6 copy-start.1
  203.8 2.6 copy-start.1
  212.0 2.6 copy-start.1
  220.2 2.6 copy-start.1
  228.4 2.6 copy-start.1
  233.3 0.7 copy-start.11
  233.3 0.7 copy-start.12
  234.3 0.7 copy-start.3
  234.3 2.9 copy-start.7
  235.0 10.0 %collective-permute-start.4 = (bf16[30,1024]{1,0:T(8,128)(2,1)S(1)}, bf16[30,1024]{1,0:T(8,128)(2,1)S(1)}, u32[]{:S(2)}, u32[]{:S(2)}) collective-permute-start(bf16[30,1024]{1,0:T(8,128)(2,1)S(1)} %slice.576), channel_id=1, source_target_pairs={{0,16},{16,32},{32,48},{48,64},{64,80},{80,96},{96,112},{112,128},... | collective-permute-start | bytes 184328 | tf_op jit(solution)/shard_map/ppermute | solution.py:31
  237.8 5.7 %collective-permute-start.2 = (bf16[15,1024]{1,0:T(8,128)(2,1)}, bf16[15,1024]{1,0:T(8,128)(2,1)}, u32[]{:S(2)}, u32[]{:S(2)}) collective-permute-start(bf16[15,1024]{1,0:T(8,128)(2,1)} %get-tuple-element.207), channel_id=1, source_target_pairs={{0,16},{16,32},{32,48},{48,64},{64,80},{80,96},{96,112},{112,128},... | collective-permute-start | bytes 92168 | tf_op jit(solution)/shard_map/ppermute | solution.py:22
  241.6 3.4 collective-permute-start.3
  243.5 22.7 %copy-start.4 = (bf16[128,1024]{1,0:T(8,128)(2,1)S(1)}, bf16[128,1024]{1,0:T(8,128)(2,1)}, u32[]{:S(2)}) copy-start(bf16[128,1024]{1,0:T(8,128)(2,1)} %copy-done.3) | copy-start | bytes 786436
  273.8 284.0 %all-reduce.5.cloned.1.call-start = ((), (), s32[]{:S(2)}) async-start(), calls=%async_computation.3 | async-start | bytes 262144 | tf_op jit(solution)/shard_map/psum | solution.py:224
Sparse Core Ops, SparseCore 0:
  12.7 67.9 all-gather.2
  84.0 59.9 all-gather.4
  273.9 140.0 all-reduce.2
  416.6 141.1 all-reduce.4
